TPU v7x, 1024 devices: a whole 8x8x8 slice. The times are simulated.
1024 devices in a mesh: grp: 16 (over y, core), blk: 64 (over x, z).
Axes of the slice: x: 8, y: 8, z: 8, core: 2. Of those that a mesh axis runs over, the one named last changes fastest.
Arguments:
- tile_values: float32 [65536, 32, 128], P(('grp', 'blk')), may hold values from 0.001 to 0.1
- tile_segments: int32 [65536], P(('grp', 'blk')), may hold values from 0 to 1023, as said below
- tile_rows: int32 [65536], P(('grp', 'blk')), may hold values from 0 to 992, as said below
- tile_counts: int32 [1024], P(('grp', 'blk')), may hold values from 32 to 64, as said below
Outputs:
- row_scales: float32 [1048576], P(('grp', 'blk'))
- column_scales: float32 [1024, 128], P(('grp', 'blk'))
Inputs may be any that keep to these rules, and one draw needn't show every extreme that they name: `tile_segments`: every segment is named by a live tile of some device; segment s belongs to group s // 64, and the 64 slots of one device name segments of one group at most 4 times. `tile_rows`: multiples of 32; on each device the first 32 slots name every band once. `tile_counts`: some device has 64 live tiles and some only 32.
All inputs are finite; a program needn't handle non-finite values.
Results may differ from a plain program's by a relative error of at most 0.0003.
Values sent between devices are 32-bit elements; how exact they have to be, the bound alone decides.
A program may use at most 32 MiB of HBM per device.

v0:
```python
import jax
import jax.numpy as jnp
from jax import lax
from jax.sharding import PartitionSpec as P

TR = 32
BANDS = 32
ITERS = 2


def per_device(tile_values, tile_segments, tile_rows, tile_counts):
    group_count = lax.axis_size("grp")
    block_count = lax.axis_size("blk")
    device_count = group_count * block_count
    tile_total = tile_values.shape[0]
    band_ids = tile_rows // TR
    slot_index = jnp.arange(tile_total, dtype=jnp.int32)
    live_mask = (slot_index < tile_counts[0]).astype(jnp.float32)
    band_index = jnp.arange(BANDS, dtype=jnp.int32)
    onehot = (band_ids[:, None] == band_index[None, :]).astype(jnp.float32)
    target = jnp.float32(BANDS * TR * device_count) / jnp.float32(128 * device_count)
    owned = None
    row_result = None
    for sweep in range(ITERS):
        if sweep == 0:
            chosen = jnp.ones((tile_total, 128), jnp.float32)
        else:
            inside = lax.all_gather(owned, "blk", axis=0, tiled=True)
            scales = lax.all_gather(inside, "grp", axis=0, tiled=True)
            chosen = scales[tile_segments]
        partial_rows = jnp.sum(tile_values * chosen[:, None, :], axis=-1) * live_mask[:, None]
        sums = jnp.dot(onehot.T, partial_rows, precision=lax.Precision.HIGHEST)
        row_result = 1.0 / sums
        weights = row_result[band_ids]
        column_part = jnp.sum(tile_values * weights[:, :, None], axis=1) * live_mask[:, None]
        column_local = jax.ops.segment_sum(column_part, tile_segments, num_segments=device_count)
        grouped = lax.psum_scatter(column_local, "grp", scatter_dimension=0, tiled=True)
        column_total = lax.psum_scatter(grouped, "blk", scatter_dimension=0, tiled=True)
        owned = target / column_total
    return (row_result.reshape(BANDS * TR), owned)


def solution(mesh):
    placed = (
        P(("grp", "blk"), None, None),
        P(("grp", "blk")),
        P(("grp", "blk")),
        P(("grp", "blk")),
    )
    return jax.shard_map(
        per_device,
        mesh=mesh,
        in_specs=placed,
        out_specs=(P(("grp", "blk")), P(("grp", "blk"), None)),
        check_vma=False,
    )
```

profile of v0, /device:TPU:8, one launch (start us, length us, event | category | flops | bytes accessed | tf_op | source)
XLA Modules:
  0.0 771.1 jit_solution(15988627009072371871)
XLA Ops:
  7.2 0.0 copy-start
  7.2 0.0 reduce-scatter.3.cloned.1.call-start
  8.0 0.7 compare_select_fusion.1
  8.6 1.6 reduce_sum.36
  10.2 0.3 convolution_divide_fusion.1
  10.5 0.6 gather_fusion
  11.1 0.0 copy-done
  11.1 0.0 copy-start.1
  11.1 0.4 multiply_reduce_fusion.2
  11.5 0.3 copy-done.1
  11.8 1.6 scatter_custom_fusion
  13.4 0.0 reduce-scatter.3.cloned.1.call-update
  13.4 0.0 reduce-scatter.5.cloned.1.call-start
  13.5 1.3 dynamic-slice
  14.8 71.4 %reduce-scatter.3.cloned.1.call-done = f32[64,128]{1,0:T(8,128)} async-done(((f32[1024,128]{1,0:T(8,128)}), f32[64,128]{1,0:T(8,128)}) %reduce-scatter.3.cloned.1.call-update) | async-done | bytes 32784 | tf_op jit(solution)/shard_map/reduce_scatter | solution.py:37
  86.2 279.7 %all-reduce = f32[64,128]{1,0:T(8,128)S(1)} all-reduce(f32[64,128]{1,0:T(8,128)} %reduce-scatter.3.cloned.1.call-done), channel_id=3, replica_groups=mesh['grp'=16,'blk'=64] {'blk'}, use_global_device_ids=true, to_apply=%region_4.5.clone | all-reduce | flops 8192 | bytes 65536
  366.0 0.6 fusion.16
  366.6 37.2 %all-gather = f32[64,1,128]{2,1,0:T(1,128)S(1)} all-gather(f32[1,1,128]{2,1,0:T(1,128)S(1)} %fusion.16), channel_id=1, replica_groups=mesh['grp'=16,'blk'=64] {'blk'}, dimensions={0}, use_global_device_ids=true | all-gather | bytes 33280 | tf_op jit(solution)/shard_map/all_gather | solution.py:28
  403.8 15.7 %all_gather.7 = f32[1024,128]{1,0:T(8,128)S(1)} all-gather(f32[64,128]{1,0:T(8,128)S(1)} %bitcast.6), channel_id=1, replica_groups=mesh['grp'=16,'blk'=64] {'grp'}, dimensions={0}, use_global_device_ids=true | all-gather | bytes 557056 | tf_op jit(solution)/shard_map/all_gather | solution.py:29
  419.5 0.6 gather_fusion.1
  420.1 0.3 multiply_reduce_fusion.1
  420.4 0.3 convolution_divide_fusion
  420.7 0.6 gather_fusion.2
  421.3 0.4 multiply_reduce_fusion
  421.7 1.6 scatter_custom_fusion.1
  423.3 0.0 reduce-scatter.5.cloned.1.call-update
  423.3 0.7 reshape.16
  424.0 59.4 %reduce-scatter.5.cloned.1.call-done = f32[64,128]{1,0:T(8,128)} async-done(((f32[1024,128]{1,0:T(8,128)}), f32[64,128]{1,0:T(8,128)}) %reduce-scatter.5.cloned.1.call-update) | async-done | bytes 32784 | tf_op jit(solution)/shard_map/reduce_scatter | solution.py:37
  483.4 279.7 %all-reduce.1 = f32[64,128]{1,0:T(8,128)S(1)} all-reduce(f32[64,128]{1,0:T(8,128)} %reduce-scatter.5.cloned.1.call-done), channel_id=5, replica_groups=mesh['grp'=16,'blk'=64] {'blk'}, use_global_device_ids=true, to_apply=%region_9.10.clone | all-reduce | flops 8192 | bytes 65536
  763.1 1.2 fusion.15
  (4 shorter events, 0.0 us)
Async XLA Ops:
  7.2 3.9 copy-start
  7.2 79.1 %reduce-scatter.3.cloned.1.call-start = ((), (), s32[]{:S(2)}) async-start(), calls=%async_computation.2 | async-start | bytes 557056 | tf_op jit(solution)/shard_map/reduce_scatter | solution.py:37
  11.1 0.7 copy-start.1
  13.4 470.0 %reduce-scatter.5.cloned.1.call-start = ((), (), s32[]{:S(2)}) async-start(), calls=%async_computation.3 | async-start | bytes 557056 | tf_op jit(solution)/shard_map/reduce_scatter | solution.py:37
Sparse Core Ops, SparseCore 0:
  13.5 72.6 reduce-scatter.2
  423.5 59.8 reduce-scatter.4
where the time goes:
time: 772 us; the launch traced here: 771 us
  blocking collectives  612 us (79%)
  waiting for transfers between devices  131 us (17%)
  between operations  14.8 us (2%)
  other arithmetic  8.41 us (1%)
    unnamed x2, blocking collectives  559 us
    reduce_scatter x2, waiting for transfers between devices, per_device(): lax.psum_scatter(column_local, 'grp', scatter_dimension=0, tiled=True)  131 us
    all_gather x1, blocking collectives, per_device(): inside = lax.all_gather(owned, 'blk', axis=0, tiled=True)  37.2 us
    all_gather x1, blocking collectives, per_device(): scales = lax.all_gather(inside, 'grp', axis=0, tiled=True)  15.7 us
  transfers between devices with their start and end apart: 2, of which 2 were waited for; matrix products, arithmetic and copies ran while one was open for 0% of the time, Pallas kernels for 0%

commit v1 on v0

v1 whole, which is shorter than its diff:
```python
import functools

import jax
import jax.numpy as jnp
from jax import lax
from jax.experimental import pallas as pl
from jax.experimental.pallas import tpu as pltpu
from jax.sharding import PartitionSpec as P

TR = 32
BANDS = 32
CAP = 4
SUB = 8
LANES = 128
CHUNKS = 8
DIRECT = True
MESH = pl.DeviceIdType.MESH
F32 = jnp.float32
BF16 = jnp.bfloat16


def iota(shape, dim):
    return lax.broadcasted_iota(jnp.int32, shape, dim)


def fiota(shape, dim):
    return iota(shape, dim).astype(F32)


def split(x):
    high = x.astype(BF16)
    rest = x - high.astype(F32)
    mid = rest.astype(BF16)
    low = (rest - mid.astype(F32)).astype(BF16)
    return high, mid, low


def pick(onehot, x, dims):
    return sum(
        lax.dot_general(onehot.astype(BF16), part, (dims, ((), ())), preferred_element_type=F32)
        for part in split(x)
    )


def pick_of(x, onehot, dims):
    return sum(
        lax.dot_general(part, onehot.astype(BF16), (dims, ((), ())), preferred_element_type=F32)
        for part in split(x)
    )


def kernel(
    groups, nx, nz, tiles,
    values_hbm, segments_hbm, rows_hbm, counts_hbm,
    rows_out, columns_out,
    values, segments, bands, counts, parts,
    send_a, recv_a, send_x, recv_x, send_z, recv_z, send_own, recv_own, send_all, recv_all, send_b, recv_b, send_c, recv_c,
    load_sem, small_sem, send_sem, recv_sem,
):
    blocks = nx * nz
    me_g = lax.axis_index("grp")
    me_b = lax.axis_index("blk")
    me_x = me_b // nz
    me_z = me_b % nz
    per = tiles // CHUNKS

    def load(q):
        part = pl.ds(q * per, per)
        return pltpu.make_async_copy(values_hbm.at[part], values.at[part], load_sem.at[q])

    smalls = [
        pltpu.make_async_copy(src, dst, small_sem.at[n])
        for n, (src, dst) in enumerate(((segments_hbm, segments), (rows_hbm, bands), (counts_hbm, counts)))
    ]
    for copy in smalls:
        copy.start()
    for q in range(CHUNKS):
        load(q).start()

    barrier = pltpu.get_barrier_semaphore()

    def others(n, me, act):
        def step(k, carry):
            act(lax.rem(me + k, n))
            return carry

        lax.fori_loop(1, n, step, 0)

    others(groups, me_g, lambda o: pl.semaphore_signal(barrier, inc=1, device_id=(o, me_b), device_id_type=MESH))
    if DIRECT:
        others(blocks, me_b, lambda o: pl.semaphore_signal(barrier, inc=1, device_id=(me_g, o), device_id_type=MESH))
        peers = groups + blocks - 2
    else:
        others(nx, me_x, lambda o: pl.semaphore_signal(barrier, inc=1, device_id=(me_g, o * nz + me_z), device_id_type=MESH))
        others(nz, me_z, lambda o: pl.semaphore_signal(barrier, inc=1, device_id=(me_g, me_x * nz + o), device_id_type=MESH))
        peers = groups + nx + nz - 3

    for copy in smalls:
        copy.wait()

    seg_row = segments[...].astype(F32)
    band_row = bands[...].astype(F32) * (1.0 / TR)
    count = counts[...].astype(F32)
    group_row = jnp.floor(seg_row * (1.0 / blocks))
    block_row = seg_row - group_row * blocks
    square = (tiles, tiles)
    down, along = iota(square, 0), iota(square, 1)

    def column(row):
        return jnp.sum(jnp.where(down == along, row, 0.0), axis=1, keepdims=True)

    group_col = column(group_row)
    band_col = column(band_row)
    same_group = group_col == group_row
    rank_row = jnp.sum(jnp.where(same_group & (down < along), 1.0, 0.0), axis=0, keepdims=True)
    place_row = group_row * SUB + rank_row
    slots = groups * SUB
    place = fiota((slots, tiles), 0)
    live_down = fiota(square, 0) < count
    live_along = fiota((slots, tiles), 1) < count
    same_band = jnp.where((band_col == band_row) & live_down, 1.0, 0.0)
    here = place_row == place
    arrange = jnp.where(here & live_along, 1.0, 0.0)
    arrange_all = jnp.where(here, 1.0, 0.0)
    block_ids = jnp.sum(jnp.where(place_row + float(CAP) == place, block_row, 0.0), axis=1, keepdims=True)

    def row_pass(scaled):
        lane = iota((TR, tiles), 1)
        total = jnp.zeros((TR, tiles), F32)
        for q in range(CHUNKS):
            if scaled is None:
                load(q).wait()
            for t in range(q * per, (q + 1) * per):
                tile = values[t]
                if scaled is not None:
                    tile = tile * scaled[t : t + 1, :]
                total = jnp.where(lane == t, jnp.sum(tile, axis=1, keepdims=True), total)
        return total

    def column_pass(weights):
        for t in range(tiles):
            parts[t : t + 1, :] = jnp.sum(values[t] * weights[:, t : t + 1], axis=0, keepdims=True)
        return pick(arrange, parts[...], ((1,), (0,)))

    def stage(n, me, stage_id, source, target, device, size):
        def act(o):
            pltpu.make_async_remote_copy(
                src_ref=source(o), dst_ref=target(me), send_sem=send_sem.at[stage_id], recv_sem=recv_sem.at[stage_id],
                device_id=device(o), device_id_type=MESH,
            ).start()

        others(n, me, act)

    def finish(n, stage_id, ref, sem):
        whole = ref.at[pl.ds(0, n - 1)]
        pltpu.make_async_copy(whole, whole, sem.at[stage_id]).wait()

    sent = []

    def exchange(n, me, stage_id, source_ref, target_ref, device, split_source=True):
        stage(
            n, me, stage_id,
            (lambda o: source_ref.at[o]) if split_source else (lambda o: source_ref),
            lambda o: target_ref.at[o], device, None,
        )
        finish(n, stage_id, target_ref, recv_sem)
        sent.append((n, stage_id, target_ref))

    in_group = lambda o: (o, me_b)
    in_block = lambda o: (me_g, o)
    in_x = lambda o: (me_g, o * nz + me_z)
    in_z = lambda o: (me_g, me_x * nz + o)

    def reduce_blocks(stage_id, dense):
        if DIRECT:
            send_x[stage_id] = dense.reshape(blocks, 1, LANES)
            recv_x[stage_id, me_b] = send_x[stage_id, me_b]
            exchange(blocks, me_b, stage_id, send_x.at[stage_id], recv_x.at[stage_id], in_block)
            return jnp.sum(recv_x[stage_id], axis=0)
        send_x[stage_id] = dense.reshape(nx, nz, LANES)
        recv_x[stage_id, me_x] = send_x[stage_id, me_x]
        exchange(nx, me_x, stage_id, send_x.at[stage_id], recv_x.at[stage_id], in_x)
        mine = jnp.sum(recv_x[stage_id], axis=0)
        send_z[stage_id] = mine.reshape(nz, 1, LANES)
        recv_z[stage_id, me_z] = send_z[stage_id, me_z]
        exchange(nz, me_z, stage_id + 2, send_z.at[stage_id], recv_z.at[stage_id], in_z)
        return jnp.sum(recv_z[stage_id], axis=0)

    def gather_blocks(own):
        send_own[...] = own
        if DIRECT:
            recv_own[me_b] = own
            exchange(blocks, me_b, 4, send_own, recv_own, in_block, False)
            return recv_own[...].reshape(blocks, LANES)
        recv_own[me_z] = own
        exchange(nz, me_z, 4, send_own, recv_own, in_z, False)
        line = recv_own[...].reshape(nz, LANES)
        send_all[...] = line
        recv_all[me_x] = line
        exchange(nx, me_x, 5, send_all, recv_all, in_x, False)
        return recv_all[...].reshape(blocks, LANES)

    target = float(BANDS * TR) / LANES

    sums = row_pass(None)
    weights = 1.0 / pick_of(sums, same_band, ((1,), (0,)))
    arranged = column_pass(weights) + block_ids * jnp.where(iota((slots, 1), 0) % SUB >= CAP, 1.0, 0.0)
    send_a[...] = arranged.reshape(groups, SUB, LANES)
    recv_a[me_g] = send_a[me_g]
    pl.semaphore_wait(barrier, peers)
    exchange(groups, me_g, 6, send_a, recv_a, in_group)

    got = recv_a[...].reshape(slots, LANES)
    ids = pltpu.roll(got, slots - CAP, 0)
    named = jnp.where((ids == fiota((slots, LANES), 1)) & (iota((slots, LANES), 0) % SUB < CAP), 1.0, 0.0)
    dense = pick(named, got, ((0,), (0,)))[:blocks]
    scale = target / reduce_blocks(0, dense)
    scales = gather_blocks(scale)
    reply = pick(named[:, :blocks], scales, ((1,), (0,)))
    send_b[...] = reply.reshape(groups, SUB, LANES)
    recv_b[me_g] = send_b[me_g]
    exchange(groups, me_g, 7, send_b, recv_b, in_group)
    chosen = pick(arrange_all, recv_b[...].reshape(slots, LANES), ((0,), (0,)))

    sums = row_pass(chosen)
    weights = 1.0 / pick_of(sums, same_band, ((1,), (0,)))
    send_c[...] = column_pass(weights).reshape(groups, SUB, LANES)
    recv_c[me_g] = send_c[me_g]
    exchange(groups, me_g, 8, send_c, recv_c, in_group)
    dense = pick(named, recv_c[...].reshape(slots, LANES), ((0,), (0,)))[:blocks]
    columns_out[...] = target / reduce_blocks(1, dense)

    fold = LANES // TR
    lines = BANDS // fold
    wide = jnp.concatenate([sums] * fold, axis=0)
    lane_part = iota((lines, LANES), 1) // TR
    band_sums = jnp.zeros((lines, LANES), F32)
    for m in range(fold):
        members = jnp.where(
            (band_row == fiota((lines, tiles), 0) * fold + m) & (fiota((lines, tiles), 1) < count), 1.0, 0.0
        )
        band_sums = jnp.where(lane_part == m, pick(members, wide, ((1,), (1,))), band_sums)
    rows_out[...] = 1.0 / band_sums

    for n, stage_id, ref in sent:
        finish(n, stage_id, ref, send_sem)


def per_device(nx, nz, tile_values, tile_segments, tile_rows, tile_counts):
    groups = lax.axis_size("grp")
    blocks = lax.axis_size("blk")
    tiles = tile_values.shape[0]
    slots = groups * SUB
    anywhere = pl.BlockSpec(memory_space=pl.ANY)
    if DIRECT:
        x_buf = [pltpu.VMEM((2, blocks, 1, LANES), F32)] * 2
        z_buf = [pltpu.VMEM((2, nz, 1, LANES), F32)] * 2
        own_buf = [pltpu.VMEM((1, LANES), F32), pltpu.VMEM((blocks, 1, LANES), F32)]
    else:
        x_buf = [pltpu.VMEM((2, nx, nz, LANES), F32)] * 2
        z_buf = [pltpu.VMEM((2, nz, 1, LANES), F32)] * 2
        own_buf = [pltpu.VMEM((1, LANES), F32), pltpu.VMEM((nz, 1, LANES), F32)]
    all_buf = [pltpu.VMEM((nz, LANES), F32), pltpu.VMEM((nx, nz, LANES), F32)]
    group_buf = pltpu.VMEM((groups, SUB, LANES), F32)
    rows, columns = pl.pallas_call(
        functools.partial(kernel, groups, nx, nz, tiles),
        out_shape=(
            jax.ShapeDtypeStruct((BANDS * TR // LANES, LANES), F32),
            jax.ShapeDtypeStruct((1, LANES), F32),
        ),
        in_specs=[anywhere] * 4,
        out_specs=(pl.BlockSpec(memory_space=pltpu.VMEM),) * 2,
        scratch_shapes=[
            pltpu.VMEM((tiles, TR, LANES), F32),
            pltpu.VMEM((1, tiles), jnp.int32),
            pltpu.VMEM((1, tiles), jnp.int32),
            pltpu.VMEM((1, 1), jnp.int32),
            pltpu.VMEM((tiles, LANES), F32),
            group_buf, group_buf,
            *x_buf, *z_buf, *own_buf, *all_buf,
            group_buf, group_buf, group_buf, group_buf,
            pltpu.SemaphoreType.DMA((CHUNKS,)),
            pltpu.SemaphoreType.DMA((3,)),
            pltpu.SemaphoreType.DMA((9,)),
            pltpu.SemaphoreType.DMA((9,)),
        ],
        compiler_params=pltpu.CompilerParams(collective_id=0, has_side_effects=True, vmem_limit_bytes=32 * 1024 * 1024),
    )(
        tile_values,
        tile_segments.reshape(1, tiles),
        tile_rows.reshape(1, tiles),
        tile_counts.reshape(1, 1),
    )
    return rows.reshape(BANDS * TR), columns


def solution(mesh):
    blocks = mesh.shape["blk"]
    nz = 8
    nx = blocks // nz
    placed = (
        P(("grp", "blk"), None, None),
        P(("grp", "blk")),
        P(("grp", "blk")),
        P(("grp", "blk")),
    )
    return jax.shard_map(
        functools.partial(per_device, nx, nz),
        mesh=mesh,
        in_specs=placed,
        out_specs=(P(("grp", "blk")), P(("grp", "blk"), None)),
        check_vma=False,
    )
```

time: 772 us -> 69.7 us (0.09)
  the two profiles are of different devices: /device:TPU:8 before, /device:TPU:1 now
where the time goes in v1:
time: 69.7 us; the launch traced here: 69.5 us
  Pallas kernels  65.2 us (94%)
  local copies, waits for them, and re-layouts  2.99 us (4%)
  between operations  1.3 us (2%)
    pallas_call x1, Pallas kernels, per_device(): pl.pallas_call(functools.partial(kernel, groups, nx, nz, tiles), out_shap...  65.2 us
    unnamed x8, local copies, waits for them, and re-layouts  2.99 us

profile of v1, /device:TPU:1, one launch (start us, length us, event | category | flops | bytes accessed | tf_op | source)
XLA Modules:
  0.0 69.5 jit_solution(4830758101919067955)
XLA Ops:
  1.3 0.0 copy-start.1
  1.3 0.0 copy-start.2
  1.3 0.6 copy-done.1
  1.9 0.0 copy-done.2
  1.9 0.0 copy-start
  2.0 1.2 %copy-done = f32[64,32,128]{2,1,0:T(8,128)S(1)} copy-done((f32[64,32,128]{2,1,0:T(8,128)S(1)}, f32[64,32,128]{2,1,0:T(8,128)}, u32[]{:S(2)}) %copy-start) | copy-done | bytes 1048600
  3.2 65.2 %shard_map.59 = (f32[8,128]{1,0:T(8,128)S(1)}, f32[1,128]{1,0:T(1,128)S(1)}) custom-call(f32[64,32,128]{2,1,0:T(8,128)S(1)} %copy-done, s32[1,64]{1,0:T(1,128)S(1)} %bitcast.6, s32[1,64]{1,0:T(1,128)S(1)} %bitcast.7, s32[1,1]{1,0:T(1,128)} %bitcast.4.counts_hbm), custom_call_target="tpu_custom_call" | custom-call | tf_op jit(solution)/shard_map/pallas_call | solution.py:265
  68.4 0.6 copy.9
  69.0 0.5 copy.10
Async XLA Ops:
  1.3 0.7 copy-start.1
  1.3 0.7 copy-start.2
  1.9 1.2 %copy-start = (f32[64,32,128]{2,1,0:T(8,128)S(1)}, f32[64,32,128]{2,1,0:T(8,128)}, u32[]{:S(2)}) copy-start(f32[64,32,128]{2,1,0:T(8,128)} %values_hbm.1) | copy-start | bytes 3145732

commit v2 on v0

v2 whole, which is shorter than its diff:
```python
import functools
import itertools

import jax
import jax.numpy as jnp
from jax import lax
from jax.experimental import pallas as pl
from jax.experimental.pallas import tpu as pltpu
from jax.sharding import PartitionSpec as P

TR = 32
BANDS = 32
CAP = 4
SUB = 8
LANES = 128
CHUNKS = 4
GREET_ALL = False
MESH = pl.DeviceIdType.MESH
F32 = jnp.float32
I32 = jnp.int32
BF16 = jnp.bfloat16
ROWS = (((1,), (0,)), ((), ()))


def iota(shape, dim):
    return lax.broadcasted_iota(I32, shape, dim)


def split(x):
    high = x.astype(BF16)
    return high, (x - high.astype(F32)).astype(BF16)


def dot(a, b, dims=ROWS):
    return lax.dot_general(a, b, dims, preferred_element_type=F32)


def total_of(terms):
    terms = list(terms)
    while len(terms) > 1:
        terms = [a + b for a, b in zip(terms[::2], terms[1::2])] + terms[len(terms) & ~1 :]
    return terms[0]


def by_distance(sizes):
    every = itertools.product(*(range(n) for n in sizes))
    return sorted(
        (step for step in every if any(step)),
        key=lambda step: (-sum(min(k, n - k) for k, n in zip(step, sizes) if n > 2), -step[-1], step),
    )


def back(steps, step, sizes):
    return steps.index(tuple((n - k) % n for k, n in zip(step, sizes)))


def kernel(
    groups, nx, nz, tiles,
    values_hbm, segments_hbm, rows_hbm, counts_hbm,
    rows_out, columns_out,
    values, segments, bands, counts, order_vmem, order,
    send_m, recv_m, send_a, recv_a, send_z, recv_z, send_x, recv_x, send_s, recv_s,
    send_b, recv_b, send_c, recv_c, send_r, recv_r,
    load_sem, small_sem, order_sem, send_sem, recv_sem,
):
    blocks = nx * nz
    half = groups // 2
    slots = groups * SUB
    me_g = lax.axis_index("grp")
    me_b = lax.axis_index("blk")
    me_y = me_g // 2
    me_x = me_b // nz
    me_z = me_b % nz
    per = tiles // CHUNKS

    group_steps = by_distance((half, 2))
    x_steps = by_distance((nx,))
    z_steps = by_distance((nz,))
    block_steps = by_distance((nx, nz))

    def group_device(step):
        return (lax.rem(me_y + step[0], half) * 2 + lax.rem(me_g + step[1], 2), me_b)

    def x_device(step):
        return (me_g, lax.rem(me_x + step[0], nx) * nz + me_z)

    def z_device(step):
        return (me_g, me_x * nz + lax.rem(me_z + step[0], nz))

    def block_device(step):
        return (me_g, lax.rem(me_x + step[0], nx) * nz + lax.rem(me_z + step[1], nz))

    def load(q):
        part = pl.ds(q * per, per)
        return pltpu.make_async_copy(values_hbm.at[part], values.at[part], load_sem.at[q])

    smalls = [
        pltpu.make_async_copy(src, dst, small_sem.at[n])
        for n, (src, dst) in enumerate(((segments_hbm, segments), (rows_hbm, bands), (counts_hbm, counts)))
    ]
    for copy in smalls:
        copy.start()
    for q in range(CHUNKS):
        load(q).start()

    empty = jnp.zeros((groups, SUB, LANES), F32)
    recv_a[...] = empty
    recv_c[...] = empty
    recv_m[...] = empty - 1.0

    barrier = pltpu.get_barrier_semaphore()
    greeted = [group_device(k) for k in group_steps]
    if GREET_ALL:
        greeted += [block_device(k) for k in block_steps]
    else:
        greeted += [z_device(k) for k in z_steps] + [x_device(k) for k in x_steps]
    for device in greeted:
        pl.semaphore_signal(barrier, inc=1, device_id=device, device_id_type=MESH)

    def send(stage, source, target, device):
        pltpu.make_async_remote_copy(
            src_ref=source, dst_ref=target, send_sem=send_sem.at[stage], recv_sem=recv_sem.at[stage],
            device_id=device, device_id_type=MESH,
        ).start()

    def finish(sem, stage, ref):
        pltpu.make_async_copy(ref, ref, sem.at[stage]).wait()

    def quad(ref):
        return ref.at[pl.ds(0, CAP)]

    def quads(ref):
        return ref.at[pl.ds(0, groups - 1), pl.ds(0, CAP)]

    def send_group(stage, source, target, n):
        step = group_steps[n]
        send(stage, quad(source.at[n]), quad(target.at[back(group_steps, step, (half, 2))]), group_device(step))

    def keep(source, target):
        target[groups - 1, :CAP] = source[groups - 1, :CAP]

    for copy in smalls:
        copy.wait()

    def at_place(code, steps, sizes):
        place = jnp.full(code.shape, len(steps), I32)
        for n, step in enumerate(steps):
            number = 0
            for k, size in zip(step, sizes):
                number = number * size + k
            place = jnp.where(code == number, n, place)
        return place

    seg = segments[...].reshape(1, tiles)
    count = counts[...].reshape(1, 1)
    group = seg // blocks
    block = seg % blocks
    group_code = (group // 2 + (half - me_y)) % half * 2 + (group + me_g) % 2
    group_row = at_place(group_code, group_steps, (half, 2)).astype(F32)
    z_place = at_place((block % nz + (nz - me_z)) % nz, z_steps, (nz,))
    block_row = (z_place * nx + block // nz).astype(F32)
    band_row = (bands[...].reshape(1, tiles) // TR).astype(F32)
    square = (tiles, tiles)
    down, along = iota(square, 0), iota(square, 1)
    diagonal = down == along

    def column(row):
        return jnp.sum(jnp.where(diagonal, row, 0.0), axis=1, keepdims=True)

    group_col = column(group_row)
    band_col = column(band_row)
    same_group = jnp.where(group_col == group_row, 1.0, 0.0)
    rank_row = jnp.sum(jnp.where(down < along, same_group, 0.0), axis=0, keepdims=True)
    rank_col = jnp.sum(jnp.where(along < down, same_group, 0.0), axis=1, keepdims=True)
    place_row = group_row * SUB + rank_row
    place_col = group_col * CAP + rank_col
    here = place_col == along.astype(F32)
    order_row = jnp.clip(jnp.sum(jnp.where(here, down, 0), axis=0, keepdims=True), 0, tiles - 1)
    order_vmem[:, :tiles] = order_row
    order_copy = pltpu.make_async_copy(order_vmem, order, order_sem)
    order_copy.start()
    slot_band = jnp.sum(jnp.where(here, band_col, 0.0), axis=0, keepdims=True)
    live_slot = order_row < count
    same_band = jnp.where((band_col == slot_band) & (down < count), 1.0, 0.0).astype(BF16)
    block_ids = jnp.sum(
        jnp.where(place_row == iota((slots, tiles), 0).astype(F32), block_row, 0.0), axis=1, keepdims=True
    )
    send_m[...] = jnp.broadcast_to(block_ids, (slots, LANES)).reshape(groups, SUB, LANES)
    keep(send_m, recv_m)

    lane = iota((TR, tiles), 1)

    def row_sums(tile_of):
        total = jnp.zeros((TR, tiles), F32)
        for t in range(tiles):
            total = jnp.where(lane == t, jnp.sum(tile_of(t), axis=1, keepdims=True), total)
        return total

    def row_scales(sums, members):
        high, low = split(sums)
        return jnp.where(live_slot, 1.0 / (dot(high, members) + dot(low, members)), 0.0)

    def column_pass(stage, weights, source, target):
        for n in range(groups):
            for k in range(CAP):
                s = n * CAP + k
                source[n, k : k + 1, :] = jnp.sum(
                    values[order[0, s]] * weights[:, s : s + 1], axis=0, keepdims=True
                )
            if n < groups - 1:
                send_group(stage, source, target, n)
        keep(source, target)

    def first(t):
        if t % per == 0:
            load(t // per).wait()
        return values[t]

    weights = row_scales(row_sums(first), same_band)
    order_copy.wait()
    pl.semaphore_wait(barrier, len(greeted))
    for n in range(groups - 1):
        send_group(0, send_m, recv_m, n)
    column_pass(1, weights, send_a, recv_a)

    slot_live_col = column(order_row.astype(F32)) < count.astype(F32)
    same_slot_band = jnp.where((column(slot_band) == slot_band) & slot_live_col, 1.0, 0.0).astype(BF16)
    finish(recv_sem, 0, quads(recv_m))
    ids = recv_m[...].reshape(slots, LANES)
    named = jnp.where(ids == iota((slots, LANES), 1).astype(F32), 1.0, 0.0)
    spread = named.T[:blocks].astype(BF16)
    named = named[:, :blocks].astype(BF16)

    def dense_of(ref):
        high, low = split(ref[...].reshape(slots, LANES))
        return dot(spread, high) + dot(spread, low)

    def others(ref):
        return ref.at[pl.ds(0, ref.shape[0] - 1)]

    finish(recv_sem, 1, quads(recv_a))
    send_z[...] = dense_of(recv_a).reshape(nz, nx, LANES)
    for n, step in enumerate(z_steps):
        send(2, send_z.at[n], recv_z.at[back(z_steps, step, (nz,))], z_device(step))
    recv_z[nz - 1] = send_z[nz - 1]
    finish(recv_sem, 2, others(recv_z))
    mine = total_of(recv_z[k] for k in range(nz))
    send_x[...] = mine
    for step in x_steps:
        send(3, send_x, recv_x.at[back(x_steps, step, (nx,))], x_device(step))
    recv_x[nx - 1] = mine
    finish(recv_sem, 3, others(recv_x))
    target = float(BANDS * TR) / LANES
    mine = target / total_of(recv_x[k] for k in range(nx))
    send_s[...] = mine
    for step in z_steps:
        send(4, send_s, recv_s.at[back(z_steps, step, (nz,))], z_device(step))
    recv_s[nz - 1] = mine
    finish(recv_sem, 4, others(recv_s))
    high, low = split(recv_s[...].reshape(blocks, LANES))
    send_b[...] = (dot(named, high) + dot(named, low)).reshape(groups, SUB, LANES)
    for n in range(groups - 1):
        send_group(5, send_b, recv_b, n)
    keep(send_b, recv_b)
    finish(recv_sem, 5, quads(recv_b))

    sums = row_sums(lambda s: values[order[0, s]] * recv_b[s // CAP, s % CAP : s % CAP + 1, :])
    column_pass(6, row_scales(sums, same_slot_band), send_c, recv_c)

    fold = LANES // TR
    lines = BANDS // fold
    high, low = split(jnp.concatenate([sums] * fold, axis=0))
    lane_part = iota((lines, LANES), 1) // TR
    band_sums = jnp.zeros((lines, LANES), F32)
    across = (((1,), (1,)), ((), ()))
    for m in range(fold):
        band = iota((lines, tiles), 0) * fold + m
        members = jnp.where((slot_band == band.astype(F32)) & live_slot, 1.0, 0.0).astype(BF16)
        band_sums = jnp.where(lane_part == m, dot(members, high, across) + dot(members, low, across), band_sums)
    rows_out[...] = 1.0 / band_sums

    finish(recv_sem, 6, quads(recv_c))
    send_r[...] = dense_of(recv_c).reshape(send_r.shape)
    z_offsets = [k for (k,) in z_steps] + [0]
    for n, step in enumerate(block_steps):
        row = z_offsets.index(step[1]) * nx + lax.rem(me_x + step[0], nx)
        send(7, send_r.at[pl.ds(row, 1)], recv_r.at[pl.ds(back(block_steps, step, (nx, nz)), 1)], block_device(step))
    recv_r[pl.ds(blocks - 1, 1)] = send_r[pl.ds((nz - 1) * nx + me_x, 1)]
    finish(recv_sem, 7, others(recv_r))
    columns_out[...] = target / jnp.sum(recv_r[...], axis=0, keepdims=True)

    for stage, ref in enumerate(
        (quads(recv_m), quads(recv_a), others(recv_z), others(recv_x), others(recv_s), quads(recv_b), quads(recv_c),
         others(recv_r))
    ):
        finish(send_sem, stage, ref)


def per_device(nx, nz, tile_values, tile_segments, tile_rows, tile_counts):
    groups = lax.axis_size("grp")
    blocks = lax.axis_size("blk")
    tiles = tile_values.shape[0]
    anywhere = pl.BlockSpec(memory_space=pltpu.HBM)
    group_buf = pltpu.VMEM((groups, SUB, LANES), F32)
    z_buf = pltpu.VMEM((nz, nx, LANES), F32)
    x_buf = pltpu.VMEM((nx, nx, LANES), F32)
    tile_buf = pltpu.VMEM((nx, LANES), F32)
    row_buf = pltpu.VMEM((blocks, LANES), F32)
    rows, columns = pl.pallas_call(
        functools.partial(kernel, groups, nx, nz, tiles),
        out_shape=(
            jax.ShapeDtypeStruct((BANDS * TR // LANES, LANES), F32),
            jax.ShapeDtypeStruct((1, LANES), F32),
        ),
        in_specs=[anywhere] * 4,
        out_specs=(pl.BlockSpec(memory_space=pltpu.VMEM),) * 2,
        scratch_shapes=[
            pltpu.VMEM((tiles, TR, LANES), F32),
            pltpu.VMEM((tiles,), I32),
            pltpu.VMEM((tiles,), I32),
            pltpu.VMEM((1,), I32),
            pltpu.VMEM((1, LANES), I32),
            pltpu.SMEM((1, LANES), I32),
            group_buf, group_buf, group_buf, group_buf,
            z_buf, z_buf, tile_buf, x_buf, tile_buf, z_buf,
            group_buf, group_buf, group_buf, group_buf,
            row_buf, row_buf,
            pltpu.SemaphoreType.DMA((CHUNKS,)),
            pltpu.SemaphoreType.DMA((3,)),
            pltpu.SemaphoreType.DMA,
            pltpu.SemaphoreType.DMA((8,)),
            pltpu.SemaphoreType.DMA((8,)),
        ],
        compiler_params=pltpu.CompilerParams(
            collective_id=0, has_side_effects=True, vmem_limit_bytes=53 * 1024 * 1024
        ),
    )(
        tile_values,
        tile_segments,
        tile_rows,
        tile_counts,
    )
    return rows.reshape(BANDS * TR), columns


def solution(mesh):
    blocks = mesh.shape["blk"]
    nz = 8
    nx = blocks // nz
    placed = (
        P(("grp", "blk"), None, None),
        P(("grp", "blk")),
        P(("grp", "blk")),
        P(("grp", "blk")),
    )
    return jax.shard_map(
        functools.partial(per_device, nx, nz),
        mesh=mesh,
        in_specs=placed,
        out_specs=(P(("grp", "blk")), P(("grp", "blk"), None)),
        check_vma=False,
    )
```

time: 772 us -> 61 us (0.08)
  the two profiles are of different devices: /device:TPU:8 before, /device:TPU:1 now
where the time goes in v2:
time: 61 us; the launch traced here: 60.8 us
  Pallas kernels  58.3 us (96%)
  between operations  1.33 us (2%)
  local copies, waits for them, and re-layouts  1.11 us (2%)
    pallas_call x1, Pallas kernels, per_device(): pl.pallas_call(functools.partial(kernel, groups, nx, nz, tiles), out_shap...  58.3 us

profile of v2, /device:TPU:1, one launch (start us, length us, event | category | flops | bytes accessed | tf_op | source)
XLA Modules:
  0.0 60.8 jit_solution(9254545421068817337)
XLA Ops:
  0.6 0.0 copy-start.1
  0.6 0.0 copy-start
  1.3 0.0 copy-done.1
  1.3 0.0 copy-done
  1.3 58.3 %shard_map.59 = (f32[8,128]{1,0:T(8,128)S(1)}, f32[1,128]{1,0:T(1,128)S(1)}) custom-call(f32[64,32,128]{2,1,0:T(8,128)} %values_hbm.1, s32[64]{0:T(128)S(1)} %copy-done, s32[64]{0:T(128)S(1)} %copy-done.1, s32[1]{0:T(128)S(6)} %copy.8.counts_hbm), custom_call_target="tpu_custom_call" | custom-call | tf_op jit(solution)/shard_map/pallas_call | solution.py:309
  59.7 0.6 copy.9
  60.3 0.5 copy.10
Async XLA Ops:
  0.6 0.7 %copy-start.1 = (s32[64]{0:T(128)S(1)}, s32[64]{0:T(128)}, u32[]{:S(2)}) copy-start(s32[64]{0:T(128)} %rows_hbm.1) | copy-start | bytes 772
  0.6 0.7 %copy-start = (s32[64]{0:T(128)S(1)}, s32[64]{0:T(128)}, u32[]{:S(2)}) copy-start(s32[64]{0:T(128)} %segments_hbm.1) | copy-start | bytes 772

commit v3 on v2

--- a/solution.py
+++ b/solution.py
@@ -56,12 +56,12 @@
 
 def kernel(
     groups, nx, nz, tiles,
-    values_hbm, segments_hbm, rows_hbm, counts_hbm,
+    values_hbm, segments, bands, counts,
     rows_out, columns_out,
-    values, segments, bands, counts, order_vmem, order,
+    values, order_vmem, order,
     send_m, recv_m, send_a, recv_a, send_z, recv_z, send_x, recv_x, send_s, recv_s,
     send_b, recv_b, send_c, recv_c, send_r, recv_r,
-    load_sem, small_sem, order_sem, send_sem, recv_sem,
+    load_sem, order_sem, send_sem, recv_sem,
 ):
     blocks = nx * nz
     half = groups // 2
@@ -94,12 +94,6 @@
         part = pl.ds(q * per, per)
         return pltpu.make_async_copy(values_hbm.at[part], values.at[part], load_sem.at[q])
 
-    smalls = [
-        pltpu.make_async_copy(src, dst, small_sem.at[n])
-        for n, (src, dst) in enumerate(((segments_hbm, segments), (rows_hbm, bands), (counts_hbm, counts)))
-    ]
-    for copy in smalls:
-        copy.start()
     for q in range(CHUNKS):
         load(q).start()
 
@@ -139,8 +133,6 @@
     def keep(source, target):
         target[groups - 1, :CAP] = source[groups - 1, :CAP]
 
-    for copy in smalls:
-        copy.wait()
 
     def at_place(code, steps, sizes):
         place = jnp.full(code.shape, len(steps), I32)
@@ -157,8 +149,7 @@
     block = seg % blocks
     group_code = (group // 2 + (half - me_y)) % half * 2 + (group + me_g) % 2
     group_row = at_place(group_code, group_steps, (half, 2)).astype(F32)
-    z_place = at_place((block % nz + (nz - me_z)) % nz, z_steps, (nz,))
-    block_row = (z_place * nx + block // nz).astype(F32)
+    block_row = (block % nz * nx + block // nz).astype(F32)
     band_row = (bands[...].reshape(1, tiles) // TR).astype(F32)
     square = (tiles, tiles)
     down, along = iota(square, 0), iota(square, 1)
@@ -238,25 +229,38 @@
     def others(ref):
         return ref.at[pl.ds(0, ref.shape[0] - 1)]
 
+    planes = nz // 2
+    target = float(BANDS * TR) / LANES
+    sums_here = me_z >= planes
     finish(recv_sem, 1, quads(recv_a))
-    send_z[...] = dense_of(recv_a).reshape(nz, nx, LANES)
-    for n, step in enumerate(z_steps):
-        send(2, send_z.at[n], recv_z.at[back(z_steps, step, (nz,))], z_device(step))
-    recv_z[nz - 1] = send_z[nz - 1]
-    finish(recv_sem, 2, others(recv_z))
-    mine = total_of(recv_z[k] for k in range(nz))
-    send_x[...] = mine
-    for step in x_steps:
-        send(3, send_x, recv_x.at[back(x_steps, step, (nx,))], x_device(step))
-    recv_x[nx - 1] = mine
-    finish(recv_sem, 3, others(recv_x))
-    target = float(BANDS * TR) / LANES
-    mine = target / total_of(recv_x[k] for k in range(nx))
-    send_s[...] = mine
-    for step in z_steps:
-        send(4, send_s, recv_s.at[back(z_steps, step, (nz,))], z_device(step))
-    recv_s[nz - 1] = mine
-    finish(recv_sem, 4, others(recv_s))
+    send_z[...] = dense_of(recv_a).reshape(send_z.shape)
+    for n in range(planes):
+
+        @pl.when(me_z != planes + n)
+        def _(n=n):
+            send(2, send_z.at[n], recv_z.at[me_z], (me_g, me_x * nz + planes + n))
+
+    @pl.when(sums_here)
+    def _():
+        recv_z[me_z] = send_z[me_z - planes]
+        finish(recv_sem, 2, others(recv_z))
+        mine = total_of(recv_z[k] for k in range(nz))
+        send_x[...] = mine
+        for step in x_steps:
+            send(3, send_x, recv_x.at[back(x_steps, step, (nx,))], x_device(step))
+        recv_x[nx - 1] = mine
+        finish(recv_sem, 3, others(recv_x))
+        mine = target / total_of(recv_x[k] for k in range(nx))
+        send_s[...] = mine
+        for step in z_steps:
+            send(4, send_s, recv_s.at[me_z - planes], z_device(step))
+        recv_s[me_z - planes] = mine
+        finish(recv_sem, 4, others(recv_s))
+
+    @pl.when(jnp.logical_not(sums_here))
+    def _():
+        finish(recv_sem, 4, recv_s)
+
     high, low = split(recv_s[...].reshape(blocks, LANES))
     send_b[...] = (dot(named, high) + dot(named, low)).reshape(groups, SUB, LANES)
     for n in range(groups - 1):
@@ -281,19 +285,25 @@
 
     finish(recv_sem, 6, quads(recv_c))
     send_r[...] = dense_of(recv_c).reshape(send_r.shape)
-    z_offsets = [k for (k,) in z_steps] + [0]
     for n, step in enumerate(block_steps):
-        row = z_offsets.index(step[1]) * nx + lax.rem(me_x + step[0], nx)
+        row = lax.rem(me_z + step[1], nz) * nx + lax.rem(me_x + step[0], nx)
         send(7, send_r.at[pl.ds(row, 1)], recv_r.at[pl.ds(back(block_steps, step, (nx, nz)), 1)], block_device(step))
-    recv_r[pl.ds(blocks - 1, 1)] = send_r[pl.ds((nz - 1) * nx + me_x, 1)]
+    recv_r[pl.ds(blocks - 1, 1)] = send_r[pl.ds(me_z * nx + me_x, 1)]
     finish(recv_sem, 7, others(recv_r))
     columns_out[...] = target / jnp.sum(recv_r[...], axis=0, keepdims=True)
 
-    for stage, ref in enumerate(
-        (quads(recv_m), quads(recv_a), others(recv_z), others(recv_x), others(recv_s), quads(recv_b), quads(recv_c),
-         others(recv_r))
-    ):
+    for stage, ref in ((0, quads(recv_m)), (1, quads(recv_a)), (5, quads(recv_b)), (6, quads(recv_c)), (7, others(recv_r))):
         finish(send_sem, stage, ref)
+
+    @pl.when(sums_here)
+    def _():
+        finish(send_sem, 2, others(send_z))
+        finish(send_sem, 3, others(recv_x))
+        finish(send_sem, 4, others(recv_z))
+
+    @pl.when(jnp.logical_not(sums_here))
+    def _():
+        finish(send_sem, 2, send_z)
 
 
 def per_device(nx, nz, tile_values, tile_segments, tile_rows, tile_counts):
@@ -302,9 +312,11 @@
     tiles = tile_values.shape[0]
     anywhere = pl.BlockSpec(memory_space=pltpu.HBM)
     group_buf = pltpu.VMEM((groups, SUB, LANES), F32)
-    z_buf = pltpu.VMEM((nz, nx, LANES), F32)
-    x_buf = pltpu.VMEM((nx, nx, LANES), F32)
-    tile_buf = pltpu.VMEM((nx, LANES), F32)
+    double = 2 * nx
+    plane_buf = pltpu.VMEM((nz // 2, double, LANES), F32)
+    z_buf = pltpu.VMEM((nz, double, LANES), F32)
+    x_buf = pltpu.VMEM((nx, double, LANES), F32)
+    tile_buf = pltpu.VMEM((double, LANES), F32)
     row_buf = pltpu.VMEM((blocks, LANES), F32)
     rows, columns = pl.pallas_call(
         functools.partial(kernel, groups, nx, nz, tiles),
@@ -312,21 +324,17 @@
             jax.ShapeDtypeStruct((BANDS * TR // LANES, LANES), F32),
             jax.ShapeDtypeStruct((1, LANES), F32),
         ),
-        in_specs=[anywhere] * 4,
+        in_specs=[anywhere] + [pl.BlockSpec(memory_space=pltpu.VMEM)] * 3,
         out_specs=(pl.BlockSpec(memory_space=pltpu.VMEM),) * 2,
         scratch_shapes=[
             pltpu.VMEM((tiles, TR, LANES), F32),
-            pltpu.VMEM((tiles,), I32),
-            pltpu.VMEM((tiles,), I32),
-            pltpu.VMEM((1,), I32),
             pltpu.VMEM((1, LANES), I32),
             pltpu.SMEM((1, LANES), I32),
             group_buf, group_buf, group_buf, group_buf,
-            z_buf, z_buf, tile_buf, x_buf, tile_buf, z_buf,
+            plane_buf, z_buf, tile_buf, x_buf, tile_buf, plane_buf,
             group_buf, group_buf, group_buf, group_buf,
             row_buf, row_buf,
             pltpu.SemaphoreType.DMA((CHUNKS,)),
-            pltpu.SemaphoreType.DMA((3,)),
             pltpu.SemaphoreType.DMA,
             pltpu.SemaphoreType.DMA((8,)),
             pltpu.SemaphoreType.DMA((8,)),

time: 61 us -> 59.3 us (0.972)
  Pallas kernels: 58.3 us -> 56.7 us
    pallas_call x1, Pallas kernels: 58.3 us -> 56.7 us  [per_device(): pl.pallas_call(functools.partial(kernel, groups, nx, nz, tiles), out_shap...]
where the time goes in v3:
time: 59.3 us; the launch traced here: 59.2 us
  Pallas kernels  56.7 us (96%)
  between operations  1.33 us (2%)
  local copies, waits for them, and re-layouts  1.11 us (2%)
    pallas_call x1, Pallas kernels, per_device(): pl.pallas_call(functools.partial(kernel, groups, nx, nz, tiles), out_shap...  56.7 us

profile of v3, /device:TPU:1, one launch (start us, length us, event | category | flops | bytes accessed | tf_op | source)
XLA Modules:
  0.0 59.2 jit_solution(17622117002607215275)
XLA Ops:
  0.6 0.0 copy-start.1
  0.6 0.0 copy-start
  1.3 0.0 copy-done.1
  1.3 0.0 copy-done
  1.3 56.7 %shard_map.59 = (f32[8,128]{1,0:T(8,128)S(1)}, f32[1,128]{1,0:T(1,128)S(1)}) custom-call(f32[64,32,128]{2,1,0:T(8,128)} %values_hbm.1, s32[64]{0:T(128)S(1)} %copy-done, s32[64]{0:T(128)S(1)} %copy-done.1, s32[1]{0:T(128)S(6)} %copy.8.counts), custom_call_target="tpu_custom_call" | custom-call | tf_op jit(solution)/shard_map/pallas_call | solution.py:321
  58.1 0.6 %copy.9 = f32[1024]{0:T(1024)} copy(f32[1024]{0:T(1024)S(1)} %bitcast.1) | data formatting | bytes 8192
  58.7 0.5 copy.10
Async XLA Ops:
  0.6 0.7 %copy-start.1 = (s32[64]{0:T(128)S(1)}, s32[64]{0:T(128)}, u32[]{:S(2)}) copy-start(s32[64]{0:T(128)} %bands.1) | copy-start | bytes 772
  0.6 0.7 %copy-start = (s32[64]{0:T(128)S(1)}, s32[64]{0:T(128)}, u32[]{:S(2)}) copy-start(s32[64]{0:T(128)} %segments.1) | copy-start | bytes 772

commit v4 on v3

--- a/solution.py
+++ b/solution.py
@@ -221,10 +221,12 @@
     named = jnp.where(ids == iota((slots, LANES), 1).astype(F32), 1.0, 0.0)
     spread = named.T[:blocks].astype(BF16)
     named = named[:, :blocks].astype(BF16)
+    spread_twice = jnp.concatenate([spread, spread], axis=1)
+    named_twice = jnp.concatenate([named, named], axis=1)
 
     def dense_of(ref):
         high, low = split(ref[...].reshape(slots, LANES))
-        return dot(spread, high) + dot(spread, low)
+        return dot(spread_twice, jnp.concatenate([high, low], axis=0))
 
     def others(ref):
         return ref.at[pl.ds(0, ref.shape[0] - 1)]
@@ -262,7 +264,7 @@
         finish(recv_sem, 4, recv_s)
 
     high, low = split(recv_s[...].reshape(blocks, LANES))
-    send_b[...] = (dot(named, high) + dot(named, low)).reshape(groups, SUB, LANES)
+    send_b[...] = dot(named_twice, jnp.concatenate([high, low], axis=0)).reshape(groups, SUB, LANES)
     for n in range(groups - 1):
         send_group(5, send_b, recv_b, n)
     keep(send_b, recv_b)

time: 59.3 us -> 59.3 us (level)
  no operation moved by 1% of the time
where the time goes in v4:
time: 59.3 us; the launch traced here: 59.2 us
  Pallas kernels  56.7 us (96%)
  between operations  1.33 us (2%)
  local copies, waits for them, and re-layouts  1.11 us (2%)
    pallas_call x1, Pallas kernels, per_device(): pl.pallas_call(functools.partial(kernel, groups, nx, nz, tiles), out_shap...  56.7 us

profile of v4, /device:TPU:1, one launch (start us, length us, event | category | flops | bytes accessed | tf_op | source)
XLA Modules:
  0.0 59.2 jit_solution(16183925821521076204)
XLA Ops:
  0.6 0.0 copy-start.1
  0.6 0.0 copy-start
  1.3 0.0 copy-done.1
  1.3 0.0 copy-done
  1.3 56.7 %shard_map.59 = (f32[8,128]{1,0:T(8,128)S(1)}, f32[1,128]{1,0:T(1,128)S(1)}) custom-call(f32[64,32,128]{2,1,0:T(8,128)} %values_hbm.1, s32[64]{0:T(128)S(1)} %copy-done, s32[64]{0:T(128)S(1)} %copy-done.1, s32[1]{0:T(128)S(6)} %copy.8.counts), custom_call_target="tpu_custom_call" | custom-call | tf_op jit(solution)/shard_map/pallas_call | solution.py:323
  58.0 0.6 %copy.9 = f32[1024]{0:T(1024)} copy(f32[1024]{0:T(1024)S(1)} %bitcast.1) | data formatting | bytes 8192
  58.6 0.5 copy.10
Async XLA Ops:
  0.6 0.7 %copy-start.1 = (s32[64]{0:T(128)S(1)}, s32[64]{0:T(128)}, u32[]{:S(2)}) copy-start(s32[64]{0:T(128)} %bands.1) | copy-start | bytes 772
  0.6 0.7 %copy-start = (s32[64]{0:T(128)S(1)}, s32[64]{0:T(128)}, u32[]{:S(2)}) copy-start(s32[64]{0:T(128)} %segments.1) | copy-start | bytes 772
